TPU v7x, 256 devices: a whole 4x4x8 slice. The times are simulated.
256 devices in a mesh: trade: 32 (over y, z_lo, core), path: 8 (over x, z_hi).
Axes of the slice: x: 4, y: 4, z: 8 (z_hi: 2, z_lo: 4; z = z_hi * 4 + z_lo), core: 2. Of those that a mesh axis runs over, the one named last changes fastest.
Arguments:
- exercise: bfloat16 [4, 1024, 32768], P(None, 'trade', 'path'), may hold values from -13 to 13, as said below
- flags: int32 [4, 1024, 32768], P(None, 'trade', 'path'), may hold values from 0 to 1
- basis: float32 [3, 16, 32768], P(None, None, 'path'), may hold values from -6 to 6
- discount: float32 [3, 32768], P(None, 'path'), may hold values from 0.8 to 1
- deflator: float32 [4, 32768], P(None, 'path'), may hold values from 0.5 to 1
- position: float32 [1024], P('trade'), may hold values from -0.5 to 0.5
- netting: int32 [1024], P('trade'), may hold values from 0 to 15
- hazard: float32 [4], replicated, may hold values from 0.2 to 1
Outputs:
- option_value: float32 [1024, 32768], P('trade', 'path')
- exposure: float32 [4, 16], replicated
- cva: float32 [16], replicated
Inputs may be any that keep to these rules, and one draw needn't show every extreme that they name: exercise is positive exactly where flags is 1.
All inputs are finite; a program needn't handle non-finite values.
Results may differ from a plain program's by a relative error of at most 0.0003.
Values sent between devices are 32-bit elements; how exact they have to be, the bound alone decides.
A program may use at most 64 MiB of HBM per device.

v0:
```python
import jax
import jax.numpy as jnp
from jax import lax
from jax.sharding import PartitionSpec as P

NS = 16


def weighted_gram(in_money_date, features):
    masked = in_money_date[:, None, :] * features[None, :, :]
    gram = lax.dot_general(
        masked, features, (((2,), (1,)), ((), ())), precision=lax.Precision.HIGHEST
    )
    return gram.reshape(gram.shape[0], -1)


def regress(gram_flat, target_sum):
    width = target_sum.shape[1]
    gram = gram_flat.reshape(gram_flat.shape[0], width, width)
    lower = jnp.linalg.cholesky(gram)
    middle = lax.linalg.triangular_solve(lower, target_sum[:, :, None], left_side=True, lower=True)
    return lax.linalg.triangular_solve(lower, middle, left_side=True, lower=True, transpose_a=True)[
        :, :, 0
    ]


def on_device(exercise, flags, basis, discount, deflator, position, netting, hazard):
    num_dates = exercise.shape[0]
    in_money = flags.astype(jnp.float32)
    set_ids = jnp.arange(NS, dtype=jnp.int32)
    set_weights = (netting[None, :] == set_ids[:, None]).astype(jnp.float32) * position[None, :]
    positive = [None] * num_dates
    option_value = jnp.zeros(exercise.shape[1:], jnp.float32)
    for date in reversed(range(num_dates)):
        payoff = exercise[date].astype(jnp.float32)
        if date == num_dates - 1:
            option_value = in_money[date] * jnp.maximum(payoff, 0.0)
        else:
            target = discount[date][None, :] * option_value
            local_rhs = jnp.einsum(
                "kp,tp->tk", basis[date], in_money[date] * target, precision=lax.Precision.HIGHEST
            )
            gram, target_sum = lax.psum(
                (weighted_gram(in_money[date], basis[date]), local_rhs), "path"
            )
            regressed = regress(gram, target_sum)
            continuation = jnp.dot(regressed, basis[date], precision=lax.Precision.HIGHEST)
            option_value = (
                in_money[date] * jnp.maximum(payoff, continuation) + (1.0 - in_money[date]) * target
            )
        netted = (
            jnp.dot(set_weights, option_value, precision=lax.Precision.HIGHEST)
            * deflator[date][None, :]
        )
        summed = lax.psum(netted, "trade")
        positive[date] = jnp.sum(jnp.maximum(summed, 0.0), axis=1)
    stacked = jnp.stack(positive)
    totals = lax.psum(stacked, "path")
    path_count = exercise.shape[2] * lax.axis_size("path")
    exposure = totals / path_count
    cva = jnp.sum(hazard[:, None] * exposure, axis=0)
    return (option_value, exposure, cva)


def solution(mesh):
    return jax.shard_map(
        on_device,
        mesh=mesh,
        in_specs=(
            P(None, "trade", "path"),
            P(None, "trade", "path"),
            P(None, None, "path"),
            P(None, "path"),
            P(None, "path"),
            P("trade"),
            P("trade"),
            P(),
        ),
        out_specs=(P("trade", "path"), P(), P()),
        check_vma=False,
    )
```

profile of v0, /device:TPU:1, one launch (start us, length us, event | category | flops | bytes accessed | tf_op | source)
XLA Modules:
  0.0 781.6 jit_solution(18033525659455575675)
XLA Ops:
  7.2 1.8 convert_element_type.27
  9.1 1.0 copy-done
  10.2 0.6 fusion.65
  10.8 30.3 %fusion = f32[32,16,16]{1,2,0:T(8,128)} fusion(f32[16,4096]{1,0:T(8,128)S(1)} %get-tuple-element.22, f32[32,4096]{1,0:T(8,128)S(1)} %get-tuple-element.18, f32[3,16,4096]{2,1,0:T(8,128)S(1)} %copy-done), kind=kOutput, calls=%fused_computation | convolution fusion | flops 404750336 | bytes 1081344 | tf_op jit(solution)/shard_map/dot_general | solution.py:11
  41.1 30.1 %fusion.2 = f32[32,16,16]{1,2,0:T(8,128)} fusion(f32[16,4096]{1,0:T(8,128)S(1)} %get-tuple-element.20, f32[32,4096]{1,0:T(8,128)S(1)} %get-tuple-element.17, f32[3,16,4096]{2,1,0:T(8,128)S(1)} %copy-done), kind=kOutput, calls=%fused_computation.2 | convolution fusion | flops 404750336 | bytes 1081344 | tf_op jit(solution)/shard_map/dot_general | solution.py:11
  71.2 30.2 %fusion.4 = f32[32,16,16]{1,2,0:T(8,128)} fusion(f32[16,4096]{1,0:T(8,128)S(1)} %get-tuple-element.21, f32[32,4096]{1,0:T(8,128)S(1)} %get-tuple-element.19, f32[3,16,4096]{2,1,0:T(8,128)S(1)} %copy-done), kind=kOutput, calls=%fused_computation.4 | convolution fusion | flops 404750336 | bytes 1081344 | tf_op jit(solution)/shard_map/dot_general | solution.py:11
  101.4 2.2 convolution_bitcast_fusion.2
  103.6 0.3 all-reduce.5.cloned.1.call-start
  103.9 0.6 iota_compare_fusion.1
  104.5 0.6 fusion.64
  105.1 2.1 convolution_multiply_fusion
  107.2 0.6 iota_compare_fusion
  107.8 119.6 %all-reduce.7.cloned.1.call-done = (f32[32,16,16]{1,2,0:T(8,128)}, f32[32,16,16]{1,2,0:T(8,128)}, f32[32,16,16]{1,2,0:T(8,128)}, f32[32,16,1]{0,1,2:T(8,128)}) async-done(((f32[32,16,16]{1,2,0:T(8,128)}, f32[32,16,16]{1,2,0:T(8,128)}, f32[32,16,16]{1,2,0:T(8,128)}, f32[32,16,1]{0,1,2:T(8,128)}), (f32[32,16,16]{1,2,0:T(8,128)}, f32[32,16,16]{1,2,0:T(8,128)}, f32[32,16,16]{1,2,0:T(8,128)}, ...) | async-done | bytes 100368 | tf_op jit(solution)/shard_map/psum | solution.py:43
  227.4 1.1 copy.28
  228.5 1.8 copy.32
  230.3 2.0 fusion.28
  232.3 47.6 %custom-call.16 = f32[32,16,16]{2,1,0:T(8,128)S(1)} custom-call(f32[32,16,16]{2,1,0:T(8,128)} %get-tuple-element.36), custom_call_target="Cholesky" | custom-call | tf_op jit(solution)/shard_map/jit(cholesky)/cholesky | solution.py:20
  280.0 48.2 %custom-call.17 = f32[32,16,16]{2,1,0:T(8,128)} custom-call(f32[32,16,16]{2,1,0:T(8,128)} %get-tuple-element.35), custom_call_target="Cholesky" | custom-call | tf_op jit(solution)/shard_map/jit(cholesky)/cholesky | solution.py:20
  328.3 1.1 copy.33
  329.4 0.8 copy.24
  330.2 1.7 fusion.32
  331.9 48.3 %custom-call.15 = f32[32,16,16]{2,1,0:T(8,128)} custom-call(f32[32,16,16]{2,1,0:T(8,128)} %fusion.32), custom_call_target="Cholesky" | custom-call | tf_op jit(solution)/shard_map/jit(cholesky)/cholesky | solution.py:20
  380.2 1.1 copy.25
  381.5 0.8 select_bitcast_fusion.2
  382.3 3.6 custom-call.19
  386.2 0.5 fusion.66
  386.7 1.7 fusion.7
  388.4 0.5 convolution_bitcast_fusion.1
  389.0 24.7 %psum.81 = f32[32,16,1]{0,1,2:T(8,128)S(1)} all-reduce(f32[32,16,1]{0,1,2:T(8,128)S(1)} %convolution_bitcast_fusion.1), channel_id=1, replica_groups=mesh['trade'=32,'path'=8] {'path'}, use_global_device_ids=true, to_apply=%region_6.10 | all-reduce | flops 512 | bytes 4096 | tf_op jit(solution)/shard_map/psum | solution.py:43
  413.7 3.6 custom-call.21
  417.6 0.5 fusion.67
  418.2 1.6 fusion.9
  419.8 1.5 convolution_bitcast_fusion
  421.3 22.3 %psum.82 = f32[32,16,1]{0,1,2:T(8,128)S(1)} all-reduce(f32[32,16,1]{0,1,2:T(8,128)S(1)} %convolution_bitcast_fusion), channel_id=1, replica_groups=mesh['trade'=32,'path'=8] {'path'}, use_global_device_ids=true, to_apply=%region_7.11 | all-reduce | flops 512 | bytes 4096 | tf_op jit(solution)/shard_map/psum | solution.py:43
  443.6 3.6 custom-call.23
  447.3 0.7 copy.63
  448.2 1.3 fusion.68
  449.4 1.7 fusion.11
  451.2 1.1 convolution_multiply_fusion.2
  452.3 1.1 convolution_multiply_fusion.1
  453.4 1.1 convolution_multiply_fusion.3
  454.5 289.1 %all-reduce.5.cloned.1.call-done = (f32[16,4096]{1,0:T(8,128)}, f32[16,4096]{1,0:T(8,128)}, f32[16,4096]{1,0:T(8,128)}, f32[16,4096]{1,0:T(8,128)}) async-done(((f32[16,4096]{1,0:T(8,128)}, f32[16,4096]{1,0:T(8,128)}, f32[16,4096]{1,0:T(8,128)}, f32[16,4096]{1,0:T(8,128)}), (f32[16,4096]{1,0:T(8,128)}, f32[16,4096]{1,0:T(8,128)}, f32[16,4096]{1,0:T(8,128)}, ...) | async-done | bytes 1048592 | tf_op jit(solution)/shard_map/psum | solution.py:55
  743.6 1.1 maximum_reduce_fusion.3
  744.7 1.1 maximum_reduce_fusion.2
  745.8 1.1 maximum_reduce_fusion.1
  746.9 1.1 maximum_reduce_fusion
  748.0 25.2 %psum.87 = f32[4,16]{1,0:T(4,128)S(1)} all-reduce(f32[4,16]{1,0:T(4,128)S(1)} %pad_maximum_fusion), channel_id=1, replica_groups=mesh['trade'=32,'path'=8] {'path'}, use_global_device_ids=true, to_apply=%region_16.20 | all-reduce | flops 64 | bytes 512 | tf_op jit(solution)/shard_map/psum | solution.py:58
  773.2 1.1 multiply_reduce_fusion
  (57 shorter events, 1.4 us)
Async XLA Ops:
  7.2 220.2 %all-reduce.7.cloned.1.call-start = ((), (), s32[]{:S(2)}) async-start(), calls=%async_computation.1 | async-start | bytes 1589248 | tf_op jit(solution)/shard_map/psum | solution.py:43
  9.0 1.1 copy-start
  9.0 1.2 copy-start.8
  10.8 90.6 %copy-start.9 = (f32[1,4096]{1,0:T(1,128)}, f32[1,4096]{1,0:T(1,128)S(1)}, u32[]{:S(2)}) copy-start(f32[1,4096]{1,0:T(1,128)S(1)} %get-tuple-element.28) | copy-start | bytes 49156
  71.2 33.2 %copy-start.4 = (f32[4,4096]{1,0:T(4,128)S(1)}, f32[4,4096]{1,0:T(4,128)}, u32[]{:S(2)}) copy-start(f32[4,4096]{1,0:T(4,128)} %param.17) | copy-start | bytes 196612
  71.2 33.9 %copy-start.11 = (f32[32]{0:T(128)S(1)}, f32[32]{0:T(128)}, u32[]{:S(2)}) copy-start(f32[32]{0:T(128)} %param.18) | copy-start | bytes 388
  71.2 33.9 %copy-start.13 = (s32[32]{0:T(128)S(1)}, s32[32]{0:T(128)}, u32[]{:S(2)}) copy-start(s32[32]{0:T(128)} %param.19) | copy-start | bytes 388
  103.6 640.0 %all-reduce.5.cloned.1.call-start = ((), (), s32[]{:S(2)}) async-start(), calls=%async_computation | async-start | bytes 2097152 | tf_op jit(solution)/shard_map/psum | solution.py:55
  227.4 102.0 %copy-start.2 = (f32[32,16,16]{1,2,0:T(8,128)S(1)}, f32[32,16,16]{1,2,0:T(8,128)}, u32[]{:S(2)}) copy-start(f32[32,16,16]{1,2,0:T(8,128)} %get-tuple-element.13) | copy-start | bytes 98308
  280.0 101.3 %copy-start.16 = (pred[16,16]{1,0:T(8,128)(4,1)S(1)}, pred[16,16]{1,0:T(8,128)(4,1)}, u32[]{:S(2)}) copy-start(pred[16,16]{1,0:T(8,128)(4,1)} %iota_compare_fusion.1) | copy-start | bytes 772
  280.0 101.4 %copy-start.15 = (pred[16,16]{1,0:T(8,128)(4,1)S(1)}, pred[16,16]{1,0:T(8,128)(4,1)}, u32[]{:S(2)}) copy-start(pred[16,16]{1,0:T(8,128)(4,1)} %iota_compare_fusion) | copy-start | bytes 772
  280.0 105.9 %copy-start.17 = (f32[32,16,1]{0,1,2:T(8,128)S(1)}, f32[32,16,1]{0,1,2:T(8,128)}, u32[]{:S(2)}) copy-start(f32[32,16,1]{0,1,2:T(8,128)} %get-tuple-element.16) | copy-start | bytes 6148
  328.3 58.5 %copy-start.10 = (f32[1,4096]{1,0:T(1,128)S(1)}, f32[1,4096]{1,0:T(1,128)}, u32[]{:S(2)}) copy-start(f32[1,4096]{1,0:T(1,128)} %copy-done.9) | copy-start | bytes 49156
  331.9 56.5 %copy-start.3 = (f32[1,4096]{1,0:T(1,128)S(1)}, f32[1,4096]{1,0:T(1,128)}, u32[]{:S(2)}) copy-start(f32[1,4096]{1,0:T(1,128)} %get-tuple-element.29) | copy-start | bytes 49156
  448.1 3.0 copy-start.7
  448.1 3.0 copy-start.12
  448.1 3.0 copy-start.14
  448.2 4.1 copy-start.6
  448.2 5.2 copy-start.5
  451.1 2.2 copy-start.1
  451.1 3.3 copy-start.18
Sparse Core Ops, SparseCore 0:
  103.7 123.6 all-reduce.6
  454.6 288.9 all-reduce.4
where the time goes:
time: 794 us; the launch traced here: 782 us
  waiting for transfers between devices  409 us (52%)
  other arithmetic  168 us (21%)
  matrix products  107 us (13%)
  blocking collectives  72.3 us (9%)
  between operations  14.8 us (2%)
  local copies, waits for them, and re-layouts  9.97 us (1%)
    psum x1, waiting for transfers between devices, on_device(): summed = lax.psum(netted, 'trade')  289 us
    another operation x8, other arithmetic, regress(): lower = jnp.linalg.cholesky(gram)  145 us
    psum x1, waiting for transfers between devices, on_device(): lax.psum((weighted_gram(in_money[date], basis[date]), local_rhs), 'path')  120 us
    dot_general x3, matrix products, weighted_gram(): lax.dot_general(masked, features, (((2,), (1,)), ((), ())), precision=lax...  90.6 us
    psum x2, blocking collectives, on_device(): lax.psum((weighted_gram(in_money[date], basis[date]), local_rhs), 'path')  47.1 us
    psum x1, blocking collectives, on_device(): totals = lax.psum(stacked, 'path')  25.2 us
  transfers between devices with their start and end apart: 2, of which 2 were waited for; matrix products, arithmetic and copies ran while one was open for 0% of the time, Pallas kernels for 0%

commit v1 on v0

v1 whole, which is shorter than its diff:
```python
import functools

import jax
import jax.numpy as jnp
from jax import lax
from jax.experimental import pallas as pl
from jax.experimental.pallas import tpu as pltpu
from jax.sharding import PartitionSpec as P

NS = 16
K = 16
CORES = 2
Y = 4
Z_LO = 4
Z_HI = 2
SLABS = K // 2 + 1
LANES = 128
MESH = pl.DeviceIdType.MESH
NT = (((1,), (1,)), ((), ()))
NN = (((1,), (0,)), ((), ()))


def split(x, count):
    parts = []
    for i in range(count):
        parts.append(x.astype(jnp.bfloat16))
        if i + 1 < count:
            x = x - parts[i].astype(jnp.float32)
    return parts


def dot(a, b, dims):
    return lax.dot_general(a, b, dims, preferred_element_type=jnp.float32)


def invert(rows):
    rows = list(rows)
    column = lax.broadcasted_iota(jnp.int32, rows[0].shape, 0)
    for i in range(K):
        pivot = 1.0 / rows[i][i : i + 1, :]
        here = column == i
        scaled = jnp.where(here, pivot, rows[i] * pivot)
        for k in range(K):
            if k != i:
                factor = rows[k][i : i + 1, :]
                rows[k] = jnp.where(here, 0.0, rows[k]) - factor * scaled
        rows[i] = scaled
    return rows


def kernel(
    members,
    exercise_hbm,
    basis_hbm,
    discount_hbm,
    deflator_hbm,
    position_hbm,
    netting_hbm,
    hazard_hbm,
    value,
    exposure_out,
    cva_out,
    exercise,
    twice,
    discount,
    deflator,
    position,
    netting,
    hazard,
    masks,
    products,
    gram_acc,
    bstack,
    rhs_acc,
    first_send,
    first_recv,
    rs_send,
    rs_recv,
    ag_send,
    ag_recv,
    full,
    inverse,
    rhs_send,
    rhs_recv,
    net,
    net1,
    sum1,
    net2,
    positive,
    ar_one,
    ar_two,
    send_sem,
    recv_sem,
    in_sem,
):
    dates, trades, paths = exercise.shape
    regs = dates - 1
    per = rs_send.shape[1] // members
    plane_size = Y * Z_LO
    path = lax.axis_index("path")
    trade = lax.axis_index("trade")
    sizes = (members // Z_HI, Z_HI, Y, Z_LO, CORES)
    me = (
        path // Z_HI,
        lax.rem(path, Z_HI),
        trade // (CORES * Z_LO),
        lax.rem(trade // CORES, Z_LO),
        lax.rem(trade, CORES),
    )
    core = me[4]
    plane = trade // CORES
    width = min(1024, paths)
    pieces = [slice(c, c + width) for c in range(0, paths, width)]

    def each_piece(body, carry=None):
        def one(c, carry):
            return body(c, pl.ds(pl.multiple_of(c * width, width), width), carry)

        return lax.fori_loop(0, paths // width, one, carry)


    copies = {}

    def have(*names):
        for name in names:
            if name in copies:
                copies.pop(name).wait()

    arrivals = []
    for d in range(regs - 1, -1, -1):
        arrivals += [(("low", d), basis_hbm.at[d], twice.at[d, pl.ds(0, K)])]
        arrivals += [(("high", d), basis_hbm.at[d], twice.at[d, pl.ds(K, K)])]
        arrivals += [(("exercise", d), exercise_hbm.at[d], exercise.at[d])]
        if d == regs - 1:
            arrivals += [(("exercise", regs), exercise_hbm.at[regs], exercise.at[regs])]
            arrivals += [("discount", discount_hbm, discount)]
            arrivals += [("position", position_hbm, position), ("netting", netting_hbm, netting)]
    arrivals += [("deflator", deflator_hbm, deflator), ("hazard", hazard_hbm, hazard)]
    for i, (name, src, dst) in enumerate(arrivals):
        copies[name] = pltpu.make_async_copy(src, dst, in_sem.at[i])
        copies[name].start()

    def offsets(*axes):
        found = [()]
        for axis, size in enumerate(sizes):
            found = [o + (i,) for o in found for i in range(size if axis in axes else 1)]
        return [o for o in found if any(o)]

    along_path, along_core, along_plane = offsets(0, 1), offsets(4), offsets(2, 3)
    along_one, along_two = offsets(1, 3, 4), offsets(0, 2)

    def place(offset):
        return [
            lax.rem(m + o, size) if o else m for m, o, size in zip(me, offset, sizes, strict=True)
        ]

    def device(at):
        x, z_hi, y, z_lo, core_of = at
        return {"trade": (y * Z_LO + z_lo) * CORES + core_of, "path": x * Z_HI + z_hi}

    barrier = pltpu.get_barrier_semaphore()
    others = set(along_path + along_core + along_plane + along_one + along_two)
    for offset in sorted(others):
        pl.semaphore_signal(
            barrier, inc=1, device_id=device(place(offset)), device_id_type=MESH
        )

    phase_of = {}

    def phase(name):
        kind, d = name if isinstance(name, tuple) else (name, 0)
        return phase_of.setdefault(kind, dates * len(phase_of)) + d

    def send(name, src, dst, at):
        i = phase(name)
        pltpu.make_async_remote_copy(
            src_ref=src,
            dst_ref=dst,
            send_sem=send_sem.at[i],
            recv_sem=recv_sem.at[i],
            device_id=device(at),
            device_id_type=MESH,
        ).start()

    def wait(name, like):
        i = phase(name)
        pltpu.make_async_copy(like, like, recv_sem.at[i]).wait()
        pltpu.make_async_copy(like, like, send_sem.at[i]).wait()

    lane = lax.broadcasted_iota(jnp.int32, (8, LANES), 1)

    def prepare(d):
        def piece(c, cut, carry):
            hi, mid, low = split(twice[d, 0:K, cut], 3)
            for i, part in enumerate((hi, mid, low, hi, mid, hi)):
                bstack[d, K * i : K * i + K, cut] = part

        each_piece(piece)

    def gram(d):
        height = SLABS * K

        def piece(c, cut, total):
            masks[:, cut] = jnp.where(
                exercise[d, :, cut].astype(jnp.float32) > 0.0, 1.0, 0.0
            ).astype(jnp.bfloat16)
            base = twice[d, 0:K, cut]
            for o in range(SLABS):
                for i, part in enumerate(split(base * twice[d, o : o + K, cut], 2)):
                    products[height * i + K * o : height * i + K * o + K, cut] = part
            return total + dot(products[:, cut], masks[:, cut], NT)

        total = each_piece(piece, jnp.zeros((2 * height, trades), jnp.float32))
        gram_acc[0:height, 0:trades] = total[0:height] + total[height : 2 * height]

    def rhs(parts):
        rhs_acc[:, 0 : 2 * trades] = parts
        part = rhs_acc[0:K, :] + rhs_acc[K : 2 * K, :] + rhs_acc[2 * K : 3 * K, :]
        part = part + pltpu.roll(part, LANES - trades, 1)
        return [part[0:8], part[8:16]]

    def pack(groups):
        tile = groups[0]
        for i, group in enumerate(groups[1:]):
            tile = jnp.where(lane < trades * (i + 1), tile, pltpu.roll(group, trades * (i + 1), 1))
        return jnp.where(lane < trades * len(groups), tile, 0.0)

    def unpack(tile, i):
        return tile if i == 0 else pltpu.roll(tile, LANES - trades * i, 1)

    def gram_groups():
        return [gram_acc[8 * g : 8 * g + 8, :] for g in range(2 * SLABS - 1)]

    def first_sends(extra):
        groups = gram_groups() + extra
        for i in range(5):
            first_send[i] = pack(groups[4 * i : 4 * i + 4])
        for offset in along_path:
            send("first", first_send, first_recv.at[path], place(offset))
        first_recv[path] = first_send[...]

    def first_groups():
        wait("first", first_recv.at[pl.ds(0, members - 1)])
        total = jnp.sum(first_recv[...], axis=0)
        return [unpack(total[g // 4], g % 4) for g in range(2 * SLABS + 1)]

    def scatter_send(d):
        groups = gram_groups()
        for i in range(members * per):
            some = groups[3 * i : 3 * i + 3]
            rs_send[d, i] = pack(some) if some else jnp.zeros((8, LANES), jnp.float32)
        for r, offset in enumerate(along_path):
            at = place(offset)
            owner = at[0] * Z_HI + at[1]
            send(("rs", d), rs_send.at[d, pl.ds(owner * per, per)], rs_recv.at[d, r], at)

    def gather_send(d):
        wait(("rs", d), rs_recv.at[d])
        ag_send[d] = rs_send[d, pl.ds(path * per, per)] + jnp.sum(rs_recv[d], axis=0)
        ag_recv[d, path] = ag_send[d]
        for offset in along_path:
            send(("ag", d), ag_send.at[d], ag_recv.at[d, path], place(offset))

    def sum_groups(d):
        wait(("ag", d), ag_recv.at[d, pl.ds(0, members - 1)])
        return [unpack(ag_recv[d, g // 3 // per, g // 3 % per], g % 3) for g in range(2 * SLABS - 1)]

    def solve_prepare(d, groups):
        for o in range(SLABS):
            for half in range(2 if o < SLABS - 1 else 1):
                rows = groups[2 * o + half]
                inside = 8 if half == 0 else 8 - o
                for first, count in ((0, inside), (inside, 8 - inside)):
                    if count:
                        k = 8 * half + first
                        j = (k + o) % K
                        some = rows[first : first + count, :]
                        full[pl.ds(K * k + j, count, stride=K + 1), :] = some
                        if o:
                            full[pl.ds(K * j + k, count, stride=K + 1), :] = some
        for k, row in enumerate(invert([full[K * k : K * k + K, :] for k in range(K)])):
            inverse[d, k] = row

    def coefficients(d, low, high):
        total = jnp.zeros((K, LANES), jnp.float32)
        for k in range(K):
            row = low[k : k + 1, :] if k < 8 else high[k - 8 : k - 7, :]
            total = total + inverse[d, k] * row
        hi, mid, rest = (part.astype(jnp.float32) for part in split(total, 3))
        stacked = jnp.concatenate(
            [hi, hi, hi, mid, mid, rest, jnp.zeros((LANES - 6 * K, LANES), jnp.float32)], axis=0
        )
        return stacked.T[0:trades, 0 : 6 * K].astype(jnp.bfloat16)

    def target(d, cut, amount):
        masked = jnp.where(
            exercise[d, :, cut].astype(jnp.float32) > 0.0, discount[d : d + 1, cut] * amount, 0.0
        )
        return dot(bstack[d, 0 : 3 * K, cut], jnp.concatenate(split(masked, 2), axis=0), NT)

    def last_value(d):
        parts = 0.0
        for cut in pieces:
            amount = jnp.maximum(exercise[d, :, cut].astype(jnp.float32), 0.0)
            value[:, cut] = amount
            parts = parts + target(d - 1, cut, amount)
        return rhs(parts)

    def step(d, coefs):
        parts = 0.0
        for cut in pieces:
            continuation = dot(coefs, bstack[d, :, cut], NN)
            payoff = exercise[d, :, cut].astype(jnp.float32)
            amount = jnp.where(
                payoff > 0.0,
                jnp.maximum(payoff, continuation),
                discount[d : d + 1, cut] * value[:, cut],
            )
            value[:, cut] = amount
            if d > 0:
                parts = parts + target(d - 1, cut, amount)
        return rhs(parts) if d > 0 else None

    def rhs_send_all(d, groups):
        rhs_send[d] = pack(groups)
        rhs_recv[d, path] = rhs_send[d]
        for offset in along_path:
            send(("rhs", d), rhs_send.at[d], rhs_recv.at[d, path], place(offset))

    def rhs_wait(d):
        wait(("rhs", d), rhs_recv.at[d, pl.ds(0, members - 1)])
        total = jnp.sum(rhs_recv[d], axis=0)
        return unpack(total, 0), unpack(total, 1)

    def set_weights():
        have("position", "netting")
        sets = lax.broadcasted_iota(jnp.int32, (NS, trades), 0)
        weights = jnp.where(netting[...] == sets, position[...], 0.0)
        return jnp.concatenate([jnp.concatenate([w, w], axis=1) for w in split(weights, 3)], axis=0)

    def netted(d, left):
        def piece(c, cut, carry):
            parts = dot(left, jnp.concatenate(split(value[:, cut], 2), axis=0), NN)
            sums = parts[0:NS] + parts[NS : 2 * NS] + parts[2 * NS : 3 * NS]
            for i in range(width // LANES):
                net[d, c * (width // LANES) + i] = sums[:, LANES * i : LANES * i + LANES]

        each_piece(piece)
        for offset in along_core:
            at = place(offset)
            send(("core", d), net.at[d, pl.ds(at[4] * plane_size, plane_size)], net1.at[d], at)

    def netted_plane(d):
        wait(("core", d), net1.at[d])
        sum1[d] = net[d, pl.ds(core * plane_size, plane_size)] + net1[d]
        for r, offset in enumerate(along_plane):
            at = place(offset)
            send(("plane", d), sum1.at[d, at[2] * Z_LO + at[3]], net2.at[d, r], at)

    def netted_end(d):
        have("deflator")
        wait(("plane", d), net2.at[d])
        total = sum1[d, plane] + jnp.sum(net2[d], axis=0)
        chunk = core * plane_size + plane
        factor = deflator[d : d + 1, pl.ds(pl.multiple_of(chunk * LANES, LANES), LANES)]
        positive[NS * d : NS * d + NS, :] = jnp.maximum(factor * total, 0.0)

    last = regs
    gram_acc[...] = jnp.zeros_like(gram_acc)
    rhs_acc[...] = jnp.zeros_like(rhs_acc)
    positive[...] = jnp.zeros_like(positive)
    have(("low", 2), ("high", 2), ("exercise", 2))
    gram(2)
    prepare(2)
    have(("exercise", last), "discount")
    extra = last_value(last)
    pl.semaphore_wait(barrier, len(others))
    first_sends(extra)
    for d in (1, 0):
        have(("low", d), ("high", d), ("exercise", d))
        prepare(d)
        gram(d)
        scatter_send(d)
    left = set_weights()
    netted(3, left)
    gather_send(1)
    gather_send(0)
    groups = first_groups()
    solve_prepare(2, groups)
    coefs = coefficients(2, *groups[-2:])
    rhs_send_all(1, step(2, coefs))
    netted(2, left)
    netted_plane(3)
    solve_prepare(1, sum_groups(1))
    coefs = coefficients(1, *rhs_wait(1))
    rhs_send_all(0, step(1, coefs))
    netted(1, left)
    netted_plane(2)
    solve_prepare(0, sum_groups(0))
    netted_plane(1)
    netted_end(3)
    coefs = coefficients(0, *rhs_wait(0))
    step(0, coefs)
    netted(0, left)
    netted_end(2)
    netted_end(1)
    netted_plane(0)
    netted_end(0)

    ones = jnp.ones((16, 2 * LANES), jnp.bfloat16)
    row = dot(ones, jnp.concatenate(split(positive[...], 2), axis=1), NT)[0:1]
    for name, along, buffer, slot in (
        ("one", along_one, ar_one, (me[1] * Z_LO + me[3]) * CORES + core),
        ("two", along_two, ar_two, me[0] * Y + me[2]),
    ):
        buffer[slot] = row
        for offset in along:
            send(name, buffer.at[slot], buffer.at[slot], place(offset))
        wait(name, buffer.at[pl.ds(0, len(along))])
        row = jnp.sum(buffer[...], axis=0)
    row = row / float(paths * members)
    have("hazard")
    credit = jnp.zeros((1, LANES), jnp.float32)
    for d in range(dates):
        exposure = row if d == 0 else pltpu.roll(row, LANES - NS * d, 1)
        exposure_out[d : d + 1, :] = exposure[:, 0:NS]
        credit = credit + hazard[:, d : d + 1] * exposure
    cva_out[...] = credit[:, 0:NS]


def on_device(members, exercise, flags, basis, discount, deflator, position, netting, hazard):
    del flags
    dates, trades, paths = exercise.shape
    regs = dates - 1
    per = -(-6 // members)
    chunks = CORES * Y * Z_LO
    plane_size = Y * Z_LO
    f32, bf16 = jnp.float32, jnp.bfloat16
    vmem = pl.BlockSpec(memory_space=pltpu.VMEM)
    tile = (8, LANES)
    phases = 8 * dates
    option_value, exposure, cva = pl.pallas_call(
        functools.partial(kernel, members),
        out_shape=(
            pltpu.VMEM((trades, paths), f32),
            pltpu.VMEM((dates, NS), f32),
            pltpu.VMEM((1, NS), f32),
        ),
        in_specs=[pl.BlockSpec(memory_space=pltpu.HBM)] * 7,
        out_specs=(vmem, vmem, vmem),
        scratch_shapes=[
            pltpu.VMEM(exercise.shape, bf16),
            pltpu.VMEM((regs, 2 * K, paths), f32),
            pltpu.VMEM(discount.shape, f32),
            pltpu.VMEM(deflator.shape, f32),
            pltpu.VMEM((1, trades), f32),
            pltpu.VMEM((1, trades), jnp.int32),
            pltpu.VMEM((1, dates), f32),
            pltpu.VMEM((trades, paths), bf16),
            pltpu.VMEM((2 * SLABS * K, paths), bf16),
            pltpu.VMEM((SLABS * K, LANES), f32),
            pltpu.VMEM((regs, 6 * K, paths), bf16),
            pltpu.VMEM((3 * K, LANES), f32),
            pltpu.VMEM((5,) + tile, f32),
            pltpu.VMEM((members, 5) + tile, f32),
            pltpu.VMEM((regs - 1, members * per) + tile, f32),
            pltpu.VMEM((regs - 1, members - 1, per) + tile, f32),
            pltpu.VMEM((regs - 1, per) + tile, f32),
            pltpu.VMEM((regs - 1, members, per) + tile, f32),
            pltpu.VMEM((K * K, LANES), f32),
            pltpu.VMEM((regs, K, K, LANES), f32),
            pltpu.VMEM((regs - 1,) + tile, f32),
            pltpu.VMEM((regs - 1, members) + tile, f32),
            pltpu.VMEM((dates, chunks, NS, LANES), f32),
            pltpu.VMEM((dates, plane_size, NS, LANES), f32),
            pltpu.VMEM((dates, plane_size, NS, LANES), f32),
            pltpu.VMEM((dates, plane_size - 1, NS, LANES), f32),
            pltpu.VMEM((LANES, LANES), f32),
            pltpu.VMEM((CORES * Z_HI * Z_LO, 1, LANES), f32),
            pltpu.VMEM((members // Z_HI * Y, 1, LANES), f32),
            pltpu.SemaphoreType.DMA((phases,)),
            pltpu.SemaphoreType.DMA((phases,)),
            pltpu.SemaphoreType.DMA((3 * regs + 6,)),
        ],
        compiler_params=pltpu.CompilerParams(
            collective_id=0, has_side_effects=True, vmem_limit_bytes=48 * 1024 * 1024
        ),
    )(
        *(
            pltpu.with_memory_space_constraint(x, pltpu.HBM)
            for x in (
                exercise,
                basis,
                discount,
                deflator,
                position.reshape(1, trades),
                netting.reshape(1, trades),
                hazard.reshape(1, dates),
            )
        )
    )
    return option_value, exposure, cva.reshape(NS)


def solution(mesh):
    return jax.shard_map(
        functools.partial(on_device, mesh.shape["path"]),
        mesh=mesh,
        in_specs=(
            P(None, "trade", "path"),
            P(None, "trade", "path"),
            P(None, None, "path"),
            P(None, "path"),
            P(None, "path"),
            P("trade"),
            P("trade"),
            P(),
        ),
        out_specs=(P("trade", "path"), P(), P()),
        check_vma=False,
    )
```

time: 794 us -> 56 us (0.07); the launches traced: 782 us -> 55.9 us
  waiting for transfers between devices: 409 us -> 0 us
  other arithmetic: 168 us -> 0 us
  matrix products: 107 us -> 0 us
  blocking collectives: 72.3 us -> 0 us
  Pallas kernels: 0 us -> 53.4 us
  between operations: 14.8 us -> 0.64 us
  local copies, waits for them, and re-layouts: 9.97 us -> 1.88 us
    psum x2 -> x0, waiting for transfers between devices: 409 us -> none  [the longest x1 289 us: on_device(): summed = lax.psum(netted, 'trade')]
    another operation x14 -> x0, other arithmetic: 157 us -> none  [the longest x8 145 us: regress(): lower = jnp.linalg.cholesky(gram)]
    dot_general x13 -> x0, matrix products: 105 us -> none  [the longest x3 90.6 us: weighted_gram(): lax.dot_general(masked, features, (((2,), (1,)), ((), ())), precision=lax...]
    psum x3 -> x0, blocking collectives: 72.3 us -> none  [the longest x2 47.1 us: on_device(): lax.psum((weighted_gram(in_money[date], basis[date]), local_rhs), 'path')]
    pallas_call x0 -> x1, Pallas kernels: none -> 53.4 us  [on_device(): pl.pallas_call(functools.partial(kernel, members), out_shape=(pltpu.VMEM(...]
  transfers between devices with their start and end apart: 2 -> 0, of which waited for: 2 -> 0; matrix products, arithmetic and copies ran while one was open for 0% -> 0% of each run, Pallas kernels for 0% -> 0%
where the time goes in v1:
time: 56 us; the launch traced here: 55.9 us
  Pallas kernels  53.4 us (95%)
  local copies, waits for them, and re-layouts  1.88 us (3%)
  between operations  0.64 us (1%)
    pallas_call x1, Pallas kernels, on_device(): pl.pallas_call(functools.partial(kernel, members), out_shape=(pltpu.VMEM(...  53.4 us
    unnamed x3, local copies, waits for them, and re-layouts  1.88 us

profile of v1, /device:TPU:1, one launch (start us, length us, event | category | flops | bytes accessed | tf_op | source)
XLA Modules:
  0.0 55.9 jit_solution(14082831352118221620)
XLA Ops:
  0.6 53.4 %shard_map.94 = (f32[32,4096]{1,0:T(8,128)S(1)}, f32[4,16]{1,0:T(4,128)S(1)}, f32[1,16]{1,0:T(1,128)S(1)}) custom-call(bf16[4,32,4096]{2,1,0:T(8,128)(2,1)} %exercise_hbm.1, f32[3,16,4096]{2,1,0:T(8,128)} %basis_hbm.1, f32[3,4096]{1,0:T(4,128)} %discount_hbm.1, f32[4,4096]{1,0:T(4,128)} %deflator_hbm.1, f32[1,32]{1,0:T(1,128)} %bitcast.5, s32[1,32]{1,0:T(1,128)} %bitcast.6, ...), custom_call_target="tpu_custom_call" | custom-call | tf_op jit(solution)/shard_map/pallas_call | solution.py:442
  54.1 0.8 %copy.13 = f32[32,4096]{1,0:T(8,128)} copy(f32[32,4096]{1,0:T(8,128)S(1)} %get-tuple-element.9) | data formatting | bytes 1048576
  54.8 0.5 copy.15
  55.4 0.6 %copy.14 = f32[4,16]{1,0:T(4,128)} copy(f32[4,16]{1,0:T(4,128)S(1)} %get-tuple-element.10) | data formatting | bytes 512

commit v2 on v1

--- a/solution.py
+++ b/solution.py
@@ -58,8 +58,7 @@
     netting_hbm,
     hazard_hbm,
     value,
-    exposure_out,
-    cva_out,
+    small,
     exercise,
     twice,
     discount,
@@ -73,7 +72,8 @@
     bstack,
     rhs_acc,
     first_send,
-    first_recv,
+    first_x,
+    first_z,
     rs_send,
     rs_recv,
     ag_send,
@@ -119,12 +119,13 @@
         return lax.fori_loop(0, paths // width, one, carry)
 
 
-    copies = {}
+    copies, here = {}, set()
 
     def have(*names):
         for name in names:
-            if name in copies:
-                copies.pop(name).wait()
+            if name not in here:
+                copies[name].wait()
+                here.add(name)
 
     arrivals = []
     for d in range(regs - 1, -1, -1):
@@ -136,9 +137,12 @@
             arrivals += [("discount", discount_hbm, discount)]
             arrivals += [("position", position_hbm, position), ("netting", netting_hbm, netting)]
     arrivals += [("deflator", deflator_hbm, deflator), ("hazard", hazard_hbm, hazard)]
-    for i, (name, src, dst) in enumerate(arrivals):
-        copies[name] = pltpu.make_async_copy(src, dst, in_sem.at[i])
-        copies[name].start()
+    def fetch(some):
+        for name, src, dst in some:
+            copies[name] = pltpu.make_async_copy(src, dst, in_sem.at[len(copies)])
+            copies[name].start()
+
+    fetch(arrivals[:5])
 
     def offsets(*axes):
         found = [()]
@@ -147,6 +151,7 @@
         return [o for o in found if any(o)]
 
     along_path, along_core, along_plane = offsets(0, 1), offsets(4), offsets(2, 3)
+    along_x, along_z_hi = offsets(0), offsets(1)
     along_one, along_two = offsets(1, 3, 4), offsets(0, 2)
 
     def place(offset):
@@ -165,6 +170,7 @@
             barrier, inc=1, device_id=device(place(offset)), device_id_type=MESH
         )
 
+    fetch(arrivals[5:])
     phase_of = {}
 
     def phase(name):
@@ -235,13 +241,20 @@
         groups = gram_groups() + extra
         for i in range(5):
             first_send[i] = pack(groups[4 * i : 4 * i + 4])
-        for offset in along_path:
-            send("first", first_send, first_recv.at[path], place(offset))
-        first_recv[path] = first_send[...]
+        first_x[me[0]] = first_send[...]
+        for offset in along_x:
+            send("first_x", first_send, first_x.at[me[0]], place(offset))
+
+    def first_sum():
+        if along_x:
+            wait("first_x", first_x.at[pl.ds(0, len(along_x))])
+        first_z[me[1]] = jnp.sum(first_x[...], axis=0)
+        for offset in along_z_hi:
+            send("first_z", first_z.at[me[1]], first_z.at[me[1]], place(offset))
 
     def first_groups():
-        wait("first", first_recv.at[pl.ds(0, members - 1)])
-        total = jnp.sum(first_recv[...], axis=0)
+        wait("first_z", first_z.at[pl.ds(0, len(along_z_hi))])
+        total = jnp.sum(first_z[...], axis=0)
         return [unpack(total[g // 4], g % 4) for g in range(2 * SLABS + 1)]
 
     def scatter_send(d):
@@ -376,19 +389,24 @@
     extra = last_value(last)
     pl.semaphore_wait(barrier, len(others))
     first_sends(extra)
-    for d in (1, 0):
+
+    def other_gram(d):
         have(("low", d), ("high", d), ("exercise", d))
         prepare(d)
         gram(d)
         scatter_send(d)
+
+    other_gram(1)
+    first_sum()
+    other_gram(0)
     left = set_weights()
     netted(3, left)
     gather_send(1)
-    gather_send(0)
     groups = first_groups()
     solve_prepare(2, groups)
     coefs = coefficients(2, *groups[-2:])
     rhs_send_all(1, step(2, coefs))
+    gather_send(0)
     netted(2, left)
     netted_plane(3)
     solve_prepare(1, sum_groups(1))
@@ -423,9 +441,24 @@
     credit = jnp.zeros((1, LANES), jnp.float32)
     for d in range(dates):
         exposure = row if d == 0 else pltpu.roll(row, LANES - NS * d, 1)
-        exposure_out[d : d + 1, :] = exposure[:, 0:NS]
+        small[d : d + 1, :] = exposure
         credit = credit + hazard[:, d : d + 1] * exposure
-    cva_out[...] = credit[:, 0:NS]
+    small[dates : dates + 1, :] = credit
+
+
+def write_results(value, small, value_out, exposure_out, cva_out, exposure, cva, sems):
+    dates = exposure.shape[0]
+    exposure[...] = small[0:dates, 0:NS]
+    cva[...] = small[dates : dates + 1, 0:NS]
+    copies = [
+        pltpu.make_async_copy(value, value_out, sems.at[0]),
+        pltpu.make_async_copy(exposure, exposure_out, sems.at[1]),
+        pltpu.make_async_copy(cva, cva_out, sems.at[2]),
+    ]
+    for copy in copies:
+        copy.start()
+    for copy in copies:
+        copy.wait()
 
 
 def on_device(members, exercise, flags, basis, discount, deflator, position, netting, hazard):
@@ -438,16 +471,15 @@
     f32, bf16 = jnp.float32, jnp.bfloat16
     vmem = pl.BlockSpec(memory_space=pltpu.VMEM)
     tile = (8, LANES)
-    phases = 8 * dates
-    option_value, exposure, cva = pl.pallas_call(
+    phases = 9 * dates
+    value, small = pl.pallas_call(
         functools.partial(kernel, members),
         out_shape=(
             pltpu.VMEM((trades, paths), f32),
-            pltpu.VMEM((dates, NS), f32),
-            pltpu.VMEM((1, NS), f32),
+            pltpu.VMEM(tile, f32),
         ),
         in_specs=[pl.BlockSpec(memory_space=pltpu.HBM)] * 7,
-        out_specs=(vmem, vmem, vmem),
+        out_specs=(vmem, vmem),
         scratch_shapes=[
             pltpu.VMEM(exercise.shape, bf16),
             pltpu.VMEM((regs, 2 * K, paths), f32),
@@ -462,7 +494,8 @@
             pltpu.VMEM((regs, 6 * K, paths), bf16),
             pltpu.VMEM((3 * K, LANES), f32),
             pltpu.VMEM((5,) + tile, f32),
-            pltpu.VMEM((members, 5) + tile, f32),
+            pltpu.VMEM((members // Z_HI, 5) + tile, f32),
+            pltpu.VMEM((Z_HI, 5) + tile, f32),
             pltpu.VMEM((regs - 1, members * per) + tile, f32),
             pltpu.VMEM((regs - 1, members - 1, per) + tile, f32),
             pltpu.VMEM((regs - 1, per) + tile, f32),
@@ -499,6 +532,23 @@
             )
         )
     )
+    hbm = pl.BlockSpec(memory_space=pltpu.HBM)
+    option_value, exposure, cva = pl.pallas_call(
+        write_results,
+        out_shape=(
+            pltpu.HBM((trades, paths), f32),
+            pltpu.HBM((dates, NS), f32),
+            pltpu.HBM((1, NS), f32),
+        ),
+        in_specs=[vmem, vmem],
+        out_specs=(hbm, hbm, hbm),
+        scratch_shapes=[
+            pltpu.VMEM((dates, NS), f32),
+            pltpu.VMEM((1, NS), f32),
+            pltpu.SemaphoreType.DMA((3,)),
+        ],
+        compiler_params=pltpu.CompilerParams(vmem_limit_bytes=1024 * 1024),
+    )(*(pltpu.with_memory_space_constraint(x, pltpu.VMEM) for x in (value, small)))
     return option_value, exposure, cva.reshape(NS)
 
 

time: 56 us -> 54.3 us (0.970)
  local copies, waits for them, and re-layouts: 1.88 us -> 0 us
    unnamed x3 -> x0, local copies, waits for them, and re-layouts: 1.88 us -> none
    pallas_call x0 -> x1, Pallas kernels: none -> 0.83 us  [on_device(): pl.pallas_call(write_results, out_shape=(pltpu.HBM((trades, paths), f32),...]
    pallas_call x1, Pallas kernels: 53.4 us -> 52.8 us  [on_device(): pl.pallas_call(functools.partial(kernel, members), out_shape=(pltpu.VMEM(...]
where the time goes in v2:
time: 54.3 us; the launch traced here: 54.2 us
  Pallas kernels  53.6 us (99%)
  between operations  0.64 us (1%)
    pallas_call x1, Pallas kernels, on_device(): pl.pallas_call(functools.partial(kernel, members), out_shape=(pltpu.VMEM(...  52.8 us

profile of v2, /device:TPU:1, one launch (start us, length us, event | category | flops | bytes accessed | tf_op | source)
XLA Modules:
  0.0 54.2 jit_solution(18169091353608319327)
XLA Ops:
  0.6 52.8 %shard_map.94 = (f32[32,4096]{1,0:T(8,128)S(1)}, f32[8,128]{1,0:T(8,128)S(1)}) custom-call(bf16[4,32,4096]{2,1,0:T(8,128)(2,1)} %exercise_hbm.1, f32[3,16,4096]{2,1,0:T(8,128)} %basis_hbm.1, f32[3,4096]{1,0:T(4,128)} %discount_hbm.1, f32[4,4096]{1,0:T(4,128)} %deflator_hbm.1, f32[1,32]{1,0:T(1,128)} %bitcast.4, s32[1,32]{1,0:T(1,128)} %bitcast.5, f32[1,4]{1,0:T(1,128)} %bitcast.6), custom_call_target="tpu_custom_call" | custom-call | tf_op jit(solution)/shard_map/pallas_call | solution.py:475
  53.4 0.8 %shard_map.95 = (f32[32,4096]{1,0:T(8,128)}, f32[4,16]{1,0:T(4,128)}, f32[1,16]{1,0:T(1,128)}) custom-call(f32[32,4096]{1,0:T(8,128)S(1)} %get-tuple-element.8.value, f32[8,128]{1,0:T(8,128)S(1)} %get-tuple-element.9.small), custom_call_target="tpu_custom_call" | custom-call | tf_op jit(solution)/shard_map/pallas_call | solution.py:536

commit v3 on v2

--- a/solution.py
+++ b/solution.py
@@ -72,8 +72,7 @@
     bstack,
     rhs_acc,
     first_send,
-    first_x,
-    first_z,
+    first_recv,
     rs_send,
     rs_recv,
     ag_send,
@@ -86,6 +85,9 @@
     net1,
     sum1,
     net2,
+    net2y,
+    sum2,
+    net3,
     positive,
     ar_one,
     ar_two,
@@ -109,15 +111,53 @@
     )
     core = me[4]
     plane = trade // CORES
-    width = min(1024, paths)
+    width = min(1024, paths // CORES)
     pieces = [slice(c, c + width) for c in range(0, paths, width)]
 
-    def each_piece(body, carry=None):
+    def each_piece(body, carry=None, unroll=False):
+        if unroll:
+            for c, cut in enumerate(pieces):
+                carry = body(c, cut, carry)
+            return carry
+
         def one(c, carry):
             return body(c, pl.ds(pl.multiple_of(c * width, width), width), carry)
 
         return lax.fori_loop(0, paths // width, one, carry)
 
+    def distance(o):
+        x, y = (min(o[i], sizes[i] - o[i]) for i in (0, 2))
+        z = abs(Z_LO * o[1] - min(o[3], Z_LO - o[3])) if o[1] else min(o[3], Z_LO - o[3])
+        return x + y + z
+
+    def offsets(*axes):
+        found = [()]
+        for axis, size in enumerate(sizes):
+            found = [o + (i,) for o in found for i in range(size if axis in axes else 1)]
+        return sorted((o for o in found if any(o)), key=distance, reverse=True)
+
+    along_path, along_core, along_plane = offsets(0, 1), offsets(4), offsets(2, 3)
+    along_y, along_z_lo = offsets(2), offsets(3)
+    along_one, along_two = offsets(1, 3, 4), offsets(0, 2)
+
+    def place(offset):
+        return [
+            lax.rem(m + o, size) if o else m for m, o, size in zip(me, offset, sizes, strict=True)
+        ]
+
+    def device(at):
+        x, z_hi, y, z_lo, core_of = at
+        return {"trade": (y * Z_LO + z_lo) * CORES + core_of, "path": x * Z_HI + z_hi}
+
+    barrier = pltpu.get_barrier_semaphore()
+
+    def greet(along):
+        for offset in along:
+            pl.semaphore_signal(
+                barrier, inc=1, device_id=device(place(offset)), device_id_type=MESH
+            )
+
+    greet(along_path)
 
     copies, here = {}, set()
 
@@ -137,40 +177,16 @@
             arrivals += [("discount", discount_hbm, discount)]
             arrivals += [("position", position_hbm, position), ("netting", netting_hbm, netting)]
     arrivals += [("deflator", deflator_hbm, deflator), ("hazard", hazard_hbm, hazard)]
+
     def fetch(some):
         for name, src, dst in some:
             copies[name] = pltpu.make_async_copy(src, dst, in_sem.at[len(copies)])
             copies[name].start()
 
     fetch(arrivals[:5])
-
-    def offsets(*axes):
-        found = [()]
-        for axis, size in enumerate(sizes):
-            found = [o + (i,) for o in found for i in range(size if axis in axes else 1)]
-        return [o for o in found if any(o)]
-
-    along_path, along_core, along_plane = offsets(0, 1), offsets(4), offsets(2, 3)
-    along_x, along_z_hi = offsets(0), offsets(1)
-    along_one, along_two = offsets(1, 3, 4), offsets(0, 2)
-
-    def place(offset):
-        return [
-            lax.rem(m + o, size) if o else m for m, o, size in zip(me, offset, sizes, strict=True)
-        ]
-
-    def device(at):
-        x, z_hi, y, z_lo, core_of = at
-        return {"trade": (y * Z_LO + z_lo) * CORES + core_of, "path": x * Z_HI + z_hi}
-
-    barrier = pltpu.get_barrier_semaphore()
-    others = set(along_path + along_core + along_plane + along_one + along_two)
-    for offset in sorted(others):
-        pl.semaphore_signal(
-            barrier, inc=1, device_id=device(place(offset)), device_id_type=MESH
-        )
-
+    greet(along_core + along_y + along_z_lo)
     fetch(arrivals[5:])
+
     phase_of = {}
 
     def phase(name):
@@ -203,7 +219,7 @@
 
         each_piece(piece)
 
-    def gram(d):
+    def gram(d, unroll=False):
         height = SLABS * K
 
         def piece(c, cut, total):
@@ -216,7 +232,7 @@
                     products[height * i + K * o : height * i + K * o + K, cut] = part
             return total + dot(products[:, cut], masks[:, cut], NT)
 
-        total = each_piece(piece, jnp.zeros((2 * height, trades), jnp.float32))
+        total = each_piece(piece, jnp.zeros((2 * height, trades), jnp.float32), unroll)
         gram_acc[0:height, 0:trades] = total[0:height] + total[height : 2 * height]
 
     def rhs(parts):
@@ -237,25 +253,18 @@
     def gram_groups():
         return [gram_acc[8 * g : 8 * g + 8, :] for g in range(2 * SLABS - 1)]
 
-    def first_sends(extra):
-        groups = gram_groups() + extra
+    def first_sends():
+        groups = gram_groups()
         for i in range(5):
             first_send[i] = pack(groups[4 * i : 4 * i + 4])
-        first_x[me[0]] = first_send[...]
-        for offset in along_x:
-            send("first_x", first_send, first_x.at[me[0]], place(offset))
-
-    def first_sum():
-        if along_x:
-            wait("first_x", first_x.at[pl.ds(0, len(along_x))])
-        first_z[me[1]] = jnp.sum(first_x[...], axis=0)
-        for offset in along_z_hi:
-            send("first_z", first_z.at[me[1]], first_z.at[me[1]], place(offset))
+        for offset in along_path:
+            send("first", first_send, first_recv.at[path], place(offset))
+        first_recv[path] = first_send[...]
 
     def first_groups():
-        wait("first_z", first_z.at[pl.ds(0, len(along_z_hi))])
-        total = jnp.sum(first_z[...], axis=0)
-        return [unpack(total[g // 4], g % 4) for g in range(2 * SLABS + 1)]
+        wait("first", first_recv.at[pl.ds(0, members - 1)])
+        total = jnp.sum(first_recv[...], axis=0)
+        return [unpack(total[g // 4], g % 4) for g in range(2 * SLABS - 1)]
 
     def scatter_send(d):
         groups = gram_groups()
@@ -319,31 +328,39 @@
             parts = parts + target(d - 1, cut, amount)
         return rhs(parts)
 
+    def new_value(d, coefs, cut):
+        continuation = dot(coefs, bstack[d, :, cut], NN)
+        payoff = exercise[d, :, cut].astype(jnp.float32)
+        amount = jnp.where(
+            payoff > 0.0,
+            jnp.maximum(payoff, continuation),
+            discount[d : d + 1, cut] * value[:, cut],
+        )
+        value[:, cut] = amount
+        return amount
+
     def step(d, coefs):
         parts = 0.0
         for cut in pieces:
-            continuation = dot(coefs, bstack[d, :, cut], NN)
-            payoff = exercise[d, :, cut].astype(jnp.float32)
-            amount = jnp.where(
-                payoff > 0.0,
-                jnp.maximum(payoff, continuation),
-                discount[d : d + 1, cut] * value[:, cut],
-            )
-            value[:, cut] = amount
-            if d > 0:
-                parts = parts + target(d - 1, cut, amount)
-        return rhs(parts) if d > 0 else None
+            parts = parts + target(d - 1, cut, new_value(d, coefs, cut))
+        return rhs(parts)
 
     def rhs_send_all(d, groups):
-        rhs_send[d] = pack(groups)
-        rhs_recv[d, path] = rhs_send[d]
+        low, high = groups
+        quarters = (low, pltpu.roll(low, 4, 0), high, pltpu.roll(high, 4, 0))
+        rhs_send[d] = pack(quarters)[0:4]
         for offset in along_path:
             send(("rhs", d), rhs_send.at[d], rhs_recv.at[d, path], place(offset))
+        rhs_recv[d, path] = rhs_send[d]
 
     def rhs_wait(d):
         wait(("rhs", d), rhs_recv.at[d, pl.ds(0, members - 1)])
         total = jnp.sum(rhs_recv[d], axis=0)
-        return unpack(total, 0), unpack(total, 1)
+        total = jnp.concatenate([total, total], axis=0)
+        upper = lax.broadcasted_iota(jnp.int32, (8, LANES), 0) < 4
+        return [
+            jnp.where(upper, unpack(total, 2 * i), unpack(total, 2 * i + 1)) for i in range(2)
+        ]
 
     def set_weights():
         have("position", "netting")
@@ -351,44 +368,94 @@
         weights = jnp.where(netting[...] == sets, position[...], 0.0)
         return jnp.concatenate([jnp.concatenate([w, w], axis=1) for w in split(weights, 3)], axis=0)
 
+    per_piece = width // LANES
+
+    def netted_piece(d, left, c, amount):
+        parts = dot(left, jnp.concatenate(split(amount, 2), axis=0), NN)
+        sums = parts[0:NS] + parts[NS : 2 * NS] + parts[2 * NS : 3 * NS]
+        for i in range(per_piece):
+            net[d, c * per_piece + i] = sums[:, LANES * i : LANES * i + LANES]
+
     def netted(d, left):
-        def piece(c, cut, carry):
-            parts = dot(left, jnp.concatenate(split(value[:, cut], 2), axis=0), NN)
-            sums = parts[0:NS] + parts[NS : 2 * NS] + parts[2 * NS : 3 * NS]
-            for i in range(width // LANES):
-                net[d, c * (width // LANES) + i] = sums[:, LANES * i : LANES * i + LANES]
-
-        each_piece(piece)
+        each_piece(lambda c, cut, carry: netted_piece(d, left, c, value[:, cut]))
         for offset in along_core:
             at = place(offset)
             send(("core", d), net.at[d, pl.ds(at[4] * plane_size, plane_size)], net1.at[d], at)
 
-    def netted_plane(d):
+    def netted_y(d):
         wait(("core", d), net1.at[d])
         sum1[d] = net[d, pl.ds(core * plane_size, plane_size)] + net1[d]
-        for r, offset in enumerate(along_plane):
+        for offset in along_y:
             at = place(offset)
-            send(("plane", d), sum1.at[d, at[2] * Z_LO + at[3]], net2.at[d, r], at)
+            send(("y", d), sum1.at[d, pl.ds(at[2] * Z_LO, Z_LO)], net2y.at[d, me[2]], at)
+        net2y[d, me[2]] = sum1[d, pl.ds(me[2] * Z_LO, Z_LO)]
+
+    def netted_z(d):
+        if along_y:
+            wait(("y", d), net2y.at[d, pl.ds(0, len(along_y))])
+        sum2[d] = jnp.sum(net2y[d], axis=0)
+        for offset in along_z_lo:
+            at = place(offset)
+            send(("z", d), sum2.at[d, at[3]], net3.at[d, me[3]], at)
+        net3[d, me[3]] = sum2[d, me[3]]
 
     def netted_end(d):
         have("deflator")
-        wait(("plane", d), net2.at[d])
-        total = sum1[d, plane] + jnp.sum(net2[d], axis=0)
+        if d == 0:
+            wait("plane", net2.at[pl.ds(0, plane_size - 1)])
+            total = jnp.sum(net2[...], axis=0)
+        else:
+            if along_z_lo:
+                wait(("z", d), net3.at[d, pl.ds(0, len(along_z_lo))])
+            total = jnp.sum(net3[d], axis=0)
         chunk = core * plane_size + plane
         factor = deflator[d : d + 1, pl.ds(pl.multiple_of(chunk * LANES, LANES), LANES)]
         positive[NS * d : NS * d + NS, :] = jnp.maximum(factor * total, 0.0)
+
+    def final_step(coefs, left):
+        half = len(pieces) // CORES
+        other = 1 - core
+        for i in range(len(pieces)):
+            c = (other if i < half else core) * half + i % half
+            cut = pl.ds(pl.multiple_of(c * width, width), width)
+            netted_piece(0, left, c, new_value(0, coefs, cut))
+            if i < half:
+                for offset in along_core:
+                    send(
+                        ("piece", i),
+                        net.at[0, pl.ds(c * per_piece, per_piece)],
+                        net1.at[0, pl.ds(i * per_piece, per_piece)],
+                        place(offset),
+                    )
+
+    def final_plane():
+        half = len(pieces) // CORES
+        for i in range(half):
+            some = slice(i * per_piece, (i + 1) * per_piece)
+            wait(("piece", i), net1.at[0, pl.ds(i * per_piece, per_piece)])
+            sum1[0, some] = (
+                net[0, pl.ds(core * plane_size + i * per_piece, per_piece)] + net1[0, some]
+            )
+            for j in range(i * per_piece, (i + 1) * per_piece):
+
+                @pl.when(j != plane)
+                def _():
+                    at = (me[0], me[1], j // Z_LO, j % Z_LO, core)
+                    send("plane", sum1.at[0, j], net2.at[plane], at)
+
+        net2[plane] = sum1[0, plane]
 
     last = regs
     gram_acc[...] = jnp.zeros_like(gram_acc)
     rhs_acc[...] = jnp.zeros_like(rhs_acc)
     positive[...] = jnp.zeros_like(positive)
     have(("low", 2), ("high", 2), ("exercise", 2))
-    gram(2)
+    gram(2, unroll=True)
+    pl.semaphore_wait(barrier, len(along_path + along_core + along_y + along_z_lo))
+    first_sends()
     prepare(2)
     have(("exercise", last), "discount")
-    extra = last_value(last)
-    pl.semaphore_wait(barrier, len(others))
-    first_sends(extra)
+    rhs_send_all(2, last_value(last))
 
     def other_gram(d):
         have(("low", d), ("high", d), ("exercise", d))
@@ -397,32 +464,32 @@
         scatter_send(d)
 
     other_gram(1)
-    first_sum()
-    other_gram(0)
     left = set_weights()
     netted(3, left)
+    other_gram(0)
+    netted_y(3)
     gather_send(1)
-    groups = first_groups()
-    solve_prepare(2, groups)
-    coefs = coefficients(2, *groups[-2:])
+    solve_prepare(2, first_groups())
+    coefs = coefficients(2, *rhs_wait(2))
     rhs_send_all(1, step(2, coefs))
     gather_send(0)
+    netted_z(3)
     netted(2, left)
-    netted_plane(3)
     solve_prepare(1, sum_groups(1))
+    netted_y(2)
     coefs = coefficients(1, *rhs_wait(1))
     rhs_send_all(0, step(1, coefs))
     netted(1, left)
-    netted_plane(2)
+    netted_z(2)
+    netted_end(3)
     solve_prepare(0, sum_groups(0))
-    netted_plane(1)
-    netted_end(3)
+    netted_y(1)
     coefs = coefficients(0, *rhs_wait(0))
-    step(0, coefs)
-    netted(0, left)
+    final_step(coefs, left)
+    netted_z(1)
     netted_end(2)
+    final_plane()
     netted_end(1)
-    netted_plane(0)
     netted_end(0)
 
     ones = jnp.ones((16, 2 * LANES), jnp.bfloat16)
@@ -471,7 +538,7 @@
     f32, bf16 = jnp.float32, jnp.bfloat16
     vmem = pl.BlockSpec(memory_space=pltpu.VMEM)
     tile = (8, LANES)
-    phases = 9 * dates
+    phases = 12 * dates
     value, small = pl.pallas_call(
         functools.partial(kernel, members),
         out_shape=(
@@ -494,20 +561,22 @@
             pltpu.VMEM((regs, 6 * K, paths), bf16),
             pltpu.VMEM((3 * K, LANES), f32),
             pltpu.VMEM((5,) + tile, f32),
-            pltpu.VMEM((members // Z_HI, 5) + tile, f32),
-            pltpu.VMEM((Z_HI, 5) + tile, f32),
+            pltpu.VMEM((members, 5) + tile, f32),
             pltpu.VMEM((regs - 1, members * per) + tile, f32),
             pltpu.VMEM((regs - 1, members - 1, per) + tile, f32),
             pltpu.VMEM((regs - 1, per) + tile, f32),
             pltpu.VMEM((regs - 1, members, per) + tile, f32),
             pltpu.VMEM((K * K, LANES), f32),
             pltpu.VMEM((regs, K, K, LANES), f32),
-            pltpu.VMEM((regs - 1,) + tile, f32),
-            pltpu.VMEM((regs - 1, members) + tile, f32),
+            pltpu.VMEM((regs, 4, LANES), f32),
+            pltpu.VMEM((regs, members, 4, LANES), f32),
             pltpu.VMEM((dates, chunks, NS, LANES), f32),
             pltpu.VMEM((dates, plane_size, NS, LANES), f32),
             pltpu.VMEM((dates, plane_size, NS, LANES), f32),
-            pltpu.VMEM((dates, plane_size - 1, NS, LANES), f32),
+            pltpu.VMEM((plane_size, NS, LANES), f32),
+            pltpu.VMEM((dates, Y, Z_LO, NS, LANES), f32),
+            pltpu.VMEM((dates, Z_LO, NS, LANES), f32),
+            pltpu.VMEM((dates, Z_LO, NS, LANES), f32),
             pltpu.VMEM((LANES, LANES), f32),
             pltpu.VMEM((CORES * Z_HI * Z_LO, 1, LANES), f32),
             pltpu.VMEM((members // Z_HI * Y, 1, LANES), f32),

time: 54.3 us -> 53.5 us (0.985)
  Pallas kernels: 53.6 us -> 52.8 us
    pallas_call x1, Pallas kernels: 52.8 us -> 51.9 us  [on_device(): pl.pallas_call(functools.partial(kernel, members), out_shape=(pltpu.VMEM(...]
where the time goes in v3:
time: 53.5 us; the launch traced here: 53.4 us
  Pallas kernels  52.8 us (99%)
  between operations  0.64 us (1%)
    pallas_call x1, Pallas kernels, on_device(): pl.pallas_call(functools.partial(kernel, members), out_shape=(pltpu.VMEM(...  51.9 us

profile of v3, /device:TPU:1, one launch (start us, length us, event | category | flops | bytes accessed | tf_op | source)
XLA Modules:
  0.0 53.4 jit_solution(711615069956451217)
XLA Ops:
  0.6 51.9 %shard_map.94 = (f32[32,4096]{1,0:T(8,128)S(1)}, f32[8,128]{1,0:T(8,128)S(1)}) custom-call(bf16[4,32,4096]{2,1,0:T(8,128)(2,1)} %exercise_hbm.1, f32[3,16,4096]{2,1,0:T(8,128)} %basis_hbm.1, f32[3,4096]{1,0:T(4,128)} %discount_hbm.1, f32[4,4096]{1,0:T(4,128)} %deflator_hbm.1, f32[1,32]{1,0:T(1,128)} %bitcast.4, s32[1,32]{1,0:T(1,128)} %bitcast.5, f32[1,4]{1,0:T(1,128)} %bitcast.6), custom_call_target="tpu_custom_call" | custom-call | tf_op jit(solution)/shard_map/pallas_call | solution.py:542
  52.6 0.8 %shard_map.95 = (f32[32,4096]{1,0:T(8,128)}, f32[4,16]{1,0:T(4,128)}, f32[1,16]{1,0:T(1,128)}) custom-call(f32[32,4096]{1,0:T(8,128)S(1)} %get-tuple-element.8.value, f32[8,128]{1,0:T(8,128)S(1)} %get-tuple-element.9.small), custom_call_target="tpu_custom_call" | custom-call | tf_op jit(solution)/shard_map/pallas_call | solution.py:605

commit v4 on v3

--- a/solution.py
+++ b/solution.py
@@ -72,7 +72,8 @@
     bstack,
     rhs_acc,
     first_send,
-    first_recv,
+    first_x,
+    first_z,
     rs_send,
     rs_recv,
     ag_send,
@@ -125,6 +126,7 @@
 
         return lax.fori_loop(0, paths // width, one, carry)
 
+
     def distance(o):
         x, y = (min(o[i], sizes[i] - o[i]) for i in (0, 2))
         z = abs(Z_LO * o[1] - min(o[3], Z_LO - o[3])) if o[1] else min(o[3], Z_LO - o[3])
@@ -137,7 +139,7 @@
         return sorted((o for o in found if any(o)), key=distance, reverse=True)
 
     along_path, along_core, along_plane = offsets(0, 1), offsets(4), offsets(2, 3)
-    along_y, along_z_lo = offsets(2), offsets(3)
+    along_x, along_z_hi, along_y, along_z_lo = offsets(0), offsets(1), offsets(2), offsets(3)
     along_one, along_two = offsets(1, 3, 4), offsets(0, 2)
 
     def place(offset):
@@ -257,13 +259,20 @@
         groups = gram_groups()
         for i in range(5):
             first_send[i] = pack(groups[4 * i : 4 * i + 4])
-        for offset in along_path:
-            send("first", first_send, first_recv.at[path], place(offset))
-        first_recv[path] = first_send[...]
+        first_x[me[0]] = first_send[...]
+        for offset in along_x:
+            send("first_x", first_send, first_x.at[me[0]], place(offset))
+
+    def first_sum():
+        if along_x:
+            wait("first_x", first_x.at[pl.ds(0, len(along_x))])
+        first_z[me[1]] = jnp.sum(first_x[...], axis=0)
+        for offset in along_z_hi:
+            send("first_z", first_z.at[me[1]], first_z.at[me[1]], place(offset))
 
     def first_groups():
-        wait("first", first_recv.at[pl.ds(0, members - 1)])
-        total = jnp.sum(first_recv[...], axis=0)
+        wait("first_z", first_z.at[pl.ds(0, len(along_z_hi))])
+        total = jnp.sum(first_z[...], axis=0)
         return [unpack(total[g // 4], g % 4) for g in range(2 * SLABS - 1)]
 
     def scatter_send(d):
@@ -436,11 +445,12 @@
             sum1[0, some] = (
                 net[0, pl.ds(core * plane_size + i * per_piece, per_piece)] + net1[0, some]
             )
-            for j in range(i * per_piece, (i + 1) * per_piece):
+            for k in range(per_piece):
+                j = i * per_piece + lax.rem(plane + k, per_piece)
 
                 @pl.when(j != plane)
-                def _():
-                    at = (me[0], me[1], j // Z_LO, j % Z_LO, core)
+                def _(j=j):
+                    at = (me[0], me[1], j // Z_LO, lax.rem(j, Z_LO), core)
                     send("plane", sum1.at[0, j], net2.at[plane], at)
 
         net2[plane] = sum1[0, plane]
@@ -464,6 +474,7 @@
         scatter_send(d)
 
     other_gram(1)
+    first_sum()
     left = set_weights()
     netted(3, left)
     other_gram(0)
@@ -561,7 +572,8 @@
             pltpu.VMEM((regs, 6 * K, paths), bf16),
             pltpu.VMEM((3 * K, LANES), f32),
             pltpu.VMEM((5,) + tile, f32),
-            pltpu.VMEM((members, 5) + tile, f32),
+            pltpu.VMEM((members // Z_HI, 5) + tile, f32),
+            pltpu.VMEM((Z_HI, 5) + tile, f32),
             pltpu.VMEM((regs - 1, members * per) + tile, f32),
             pltpu.VMEM((regs - 1, members - 1, per) + tile, f32),
             pltpu.VMEM((regs - 1, per) + tile, f32),

time: 53.5 us -> 52.9 us (0.989)
  Pallas kernels: 52.8 us -> 52.2 us
    pallas_call x1, Pallas kernels: 51.9 us -> 51.3 us  [on_device(): pl.pallas_call(functools.partial(kernel, members), out_shape=(pltpu.VMEM(...]
where the time goes in v4:
time: 52.9 us; the launch traced here: 52.8 us
  Pallas kernels  52.2 us (99%)
  between operations  0.64 us (1%)
    pallas_call x1, Pallas kernels, on_device(): pl.pallas_call(functools.partial(kernel, members), out_shape=(pltpu.VMEM(...  51.3 us

profile of v4, /device:TPU:1, one launch (start us, length us, event | category | flops | bytes accessed | tf_op | source)
XLA Modules:
  0.0 52.8 jit_solution(9577561093658180729)
XLA Ops:
  0.6 51.3 %shard_map.94 = (f32[32,4096]{1,0:T(8,128)S(1)}, f32[8,128]{1,0:T(8,128)S(1)}) custom-call(bf16[4,32,4096]{2,1,0:T(8,128)(2,1)} %exercise_hbm.1, f32[3,16,4096]{2,1,0:T(8,128)} %basis_hbm.1, f32[3,4096]{1,0:T(4,128)} %discount_hbm.1, f32[4,4096]{1,0:T(4,128)} %deflator_hbm.1, f32[1,32]{1,0:T(1,128)} %bitcast.4, s32[1,32]{1,0:T(1,128)} %bitcast.5, f32[1,4]{1,0:T(1,128)} %bitcast.6), custom_call_target="tpu_custom_call" | custom-call | tf_op jit(solution)/shard_map/pallas_call | solution.py:553
  52.0 0.8 %shard_map.95 = (f32[32,4096]{1,0:T(8,128)}, f32[4,16]{1,0:T(4,128)}, f32[1,16]{1,0:T(1,128)}) custom-call(f32[32,4096]{1,0:T(8,128)S(1)} %get-tuple-element.8.value, f32[8,128]{1,0:T(8,128)S(1)} %get-tuple-element.9.small), custom_call_target="tpu_custom_call" | custom-call | tf_op jit(solution)/shard_map/pallas_call | solution.py:617

commit v5 on v4

--- a/solution.py
+++ b/solution.py
@@ -14,6 +14,7 @@
 Z_LO = 4
 Z_HI = 2
 SLABS = K // 2 + 1
+OWNERS = 5
 LANES = 128
 MESH = pl.DeviceIdType.MESH
 NT = (((1,), (1,)), ((), ()))
@@ -76,7 +77,6 @@
     first_z,
     rs_send,
     rs_recv,
-    ag_send,
     ag_recv,
     full,
     inverse,
@@ -98,7 +98,6 @@
 ):
     dates, trades, paths = exercise.shape
     regs = dates - 1
-    per = rs_send.shape[1] // members
     plane_size = Y * Z_LO
     path = lax.axis_index("path")
     trade = lax.axis_index("trade")
@@ -206,10 +205,15 @@
             device_id_type=MESH,
         ).start()
 
+    def wait_in(name, like):
+        pltpu.make_async_copy(like, like, recv_sem.at[phase(name)]).wait()
+
+    def wait_out(name, like):
+        pltpu.make_async_copy(like, like, send_sem.at[phase(name)]).wait()
+
     def wait(name, like):
-        i = phase(name)
-        pltpu.make_async_copy(like, like, recv_sem.at[i]).wait()
-        pltpu.make_async_copy(like, like, send_sem.at[i]).wait()
+        wait_in(name, like)
+        wait_out(name, like)
 
     lane = lax.broadcasted_iota(jnp.int32, (8, LANES), 1)
 
@@ -277,24 +281,40 @@
 
     def scatter_send(d):
         groups = gram_groups()
-        for i in range(members * per):
-            some = groups[3 * i : 3 * i + 3]
-            rs_send[d, i] = pack(some) if some else jnp.zeros((8, LANES), jnp.float32)
+        for i in range(OWNERS):
+            rs_send[d, i] = pack(groups[4 * i : 4 * i + 4])
         for r, offset in enumerate(along_path):
             at = place(offset)
             owner = at[0] * Z_HI + at[1]
-            send(("rs", d), rs_send.at[d, pl.ds(owner * per, per)], rs_recv.at[d, r], at)
+
+            @pl.when(owner < OWNERS)
+            def _(r=r, at=at, owner=owner):
+                send(("rs", d), rs_send.at[d, owner], rs_recv.at[d, r], at)
 
     def gather_send(d):
-        wait(("rs", d), rs_recv.at[d])
-        ag_send[d] = rs_send[d, pl.ds(path * per, per)] + jnp.sum(rs_recv[d], axis=0)
-        ag_recv[d, path] = ag_send[d]
-        for offset in along_path:
-            send(("ag", d), ag_send.at[d], ag_recv.at[d, path], place(offset))
+        @pl.when(path < OWNERS)
+        def _():
+            wait_in(("rs", d), rs_recv.at[d])
+            ag_recv[d, path] = rs_send[d, path] + jnp.sum(rs_recv[d], axis=0)
+            for offset in along_path:
+                send(("ag", d), ag_recv.at[d, path], ag_recv.at[d, path], place(offset))
+            wait_out(("rs", d), rs_send.at[d, pl.ds(0, OWNERS - 1)])
+
+        @pl.when(path >= OWNERS)
+        def _():
+            wait_out(("rs", d), rs_send.at[d])
 
     def sum_groups(d):
-        wait(("ag", d), ag_recv.at[d, pl.ds(0, members - 1)])
-        return [unpack(ag_recv[d, g // 3 // per, g // 3 % per], g % 3) for g in range(2 * SLABS - 1)]
+        @pl.when(path < OWNERS)
+        def _():
+            wait_in(("ag", d), ag_recv.at[d, pl.ds(0, OWNERS - 1)])
+            wait_out(("ag", d), rs_recv.at[d])
+
+        @pl.when(path >= OWNERS)
+        def _():
+            wait_in(("ag", d), ag_recv.at[d])
+
+        return [unpack(ag_recv[d, g // 4], g % 4) for g in range(2 * SLABS - 1)]
 
     def solve_prepare(d, groups):
         for o in range(SLABS):
@@ -411,7 +431,8 @@
     def netted_end(d):
         have("deflator")
         if d == 0:
-            wait("plane", net2.at[pl.ds(0, plane_size - 1)])
+            if along_plane:
+                wait("plane", net2.at[pl.ds(0, plane_size - 1)])
             total = jnp.sum(net2[...], axis=0)
         else:
             if along_z_lo:
@@ -483,18 +504,18 @@
     solve_prepare(2, first_groups())
     coefs = coefficients(2, *rhs_wait(2))
     rhs_send_all(1, step(2, coefs))
-    gather_send(0)
-    netted_z(3)
     netted(2, left)
     solve_prepare(1, sum_groups(1))
     netted_y(2)
+    gather_send(0)
+    netted_z(3)
     coefs = coefficients(1, *rhs_wait(1))
     rhs_send_all(0, step(1, coefs))
     netted(1, left)
-    netted_z(2)
     netted_end(3)
     solve_prepare(0, sum_groups(0))
     netted_y(1)
+    netted_z(2)
     coefs = coefficients(0, *rhs_wait(0))
     final_step(coefs, left)
     netted_z(1)
@@ -543,7 +564,6 @@
     del flags
     dates, trades, paths = exercise.shape
     regs = dates - 1
-    per = -(-6 // members)
     chunks = CORES * Y * Z_LO
     plane_size = Y * Z_LO
     f32, bf16 = jnp.float32, jnp.bfloat16
@@ -574,10 +594,9 @@
             pltpu.VMEM((5,) + tile, f32),
             pltpu.VMEM((members // Z_HI, 5) + tile, f32),
             pltpu.VMEM((Z_HI, 5) + tile, f32),
-            pltpu.VMEM((regs - 1, members * per) + tile, f32),
-            pltpu.VMEM((regs - 1, members - 1, per) + tile, f32),
-            pltpu.VMEM((regs - 1, per) + tile, f32),
-            pltpu.VMEM((regs - 1, members, per) + tile, f32),
+            pltpu.VMEM((regs - 1, OWNERS) + tile, f32),
+            pltpu.VMEM((regs - 1, members - 1) + tile, f32),
+            pltpu.VMEM((regs - 1, OWNERS) + tile, f32),
             pltpu.VMEM((K * K, LANES), f32),
             pltpu.VMEM((regs, K, K, LANES), f32),
             pltpu.VMEM((regs, 4, LANES), f32),

time: 52.9 us -> 52.8 us (level)
  no operation moved by 1% of the time
where the time goes in v5:
time: 52.8 us; the launch traced here: 52.7 us
  Pallas kernels  52 us (98%)
  between operations  0.64 us (1%)
    pallas_call x1, Pallas kernels, on_device(): pl.pallas_call(functools.partial(kernel, members), out_shape=(pltpu.VMEM(...  51.2 us

profile of v5, /device:TPU:1, one launch (start us, length us, event | category | flops | bytes accessed | tf_op | source)
XLA Modules:
  0.0 52.7 jit_solution(11534794331759869741)
XLA Ops:
  0.6 51.2 %shard_map.94 = (f32[32,4096]{1,0:T(8,128)S(1)}, f32[8,128]{1,0:T(8,128)S(1)}) custom-call(bf16[4,32,4096]{2,1,0:T(8,128)(2,1)} %exercise_hbm.1, f32[3,16,4096]{2,1,0:T(8,128)} %basis_hbm.1, f32[3,4096]{1,0:T(4,128)} %discount_hbm.1, f32[4,4096]{1,0:T(4,128)} %deflator_hbm.1, f32[1,32]{1,0:T(1,128)} %bitcast.4, s32[1,32]{1,0:T(1,128)} %bitcast.5, f32[1,4]{1,0:T(1,128)} %bitcast.6), custom_call_target="tpu_custom_call" | custom-call | tf_op jit(solution)/shard_map/pallas_call | solution.py:573
  51.9 0.8 %shard_map.95 = (f32[32,4096]{1,0:T(8,128)}, f32[4,16]{1,0:T(4,128)}, f32[1,16]{1,0:T(1,128)}) custom-call(f32[32,4096]{1,0:T(8,128)S(1)} %get-tuple-element.8.value, f32[8,128]{1,0:T(8,128)S(1)} %get-tuple-element.9.small), custom_call_target="tpu_custom_call" | custom-call | tf_op jit(solution)/shard_map/pallas_call | solution.py:636

commit v6 on v5

--- a/solution.py
+++ b/solution.py
@@ -211,9 +211,15 @@
     def wait_out(name, like):
         pltpu.make_async_copy(like, like, send_sem.at[phase(name)]).wait()
 
+    leaving = []
+
     def wait(name, like):
         wait_in(name, like)
-        wait_out(name, like)
+        leaving.append((name, like))
+
+    def flush():
+        while leaving:
+            wait_out(*leaving.pop(0))
 
     lane = lax.broadcasted_iota(jnp.int32, (8, LANES), 1)
 
@@ -522,6 +528,7 @@
     netted_end(2)
     final_plane()
     netted_end(1)
+    flush()
     netted_end(0)
 
     ones = jnp.ones((16, 2 * LANES), jnp.bfloat16)
@@ -543,6 +550,7 @@
         small[d : d + 1, :] = exposure
         credit = credit + hazard[:, d : d + 1] * exposure
     small[dates : dates + 1, :] = credit
+    flush()
 
 
 def write_results(value, small, value_out, exposure_out, cva_out, exposure, cva, sems):

time: 52.8 us -> 52.8 us (level)
  no operation moved by 1% of the time
where the time goes in v6:
time: 52.8 us; the launch traced here: 52.7 us
  Pallas kernels  52 us (98%)
  between operations  0.64 us (1%)
    pallas_call x1, Pallas kernels, on_device(): pl.pallas_call(functools.partial(kernel, members), out_shape=(pltpu.VMEM(...  51.2 us

profile of v6, /device:TPU:1, one launch (start us, length us, event | category | flops | bytes accessed | tf_op | source)
XLA Modules:
  0.0 52.7 jit_solution(8720975976583199151)
XLA Ops:
  0.6 51.2 %shard_map.94 = (f32[32,4096]{1,0:T(8,128)S(1)}, f32[8,128]{1,0:T(8,128)S(1)}) custom-call(bf16[4,32,4096]{2,1,0:T(8,128)(2,1)} %exercise_hbm.1, f32[3,16,4096]{2,1,0:T(8,128)} %basis_hbm.1, f32[3,4096]{1,0:T(4,128)} %discount_hbm.1, f32[4,4096]{1,0:T(4,128)} %deflator_hbm.1, f32[1,32]{1,0:T(1,128)} %bitcast.4, s32[1,32]{1,0:T(1,128)} %bitcast.5, f32[1,4]{1,0:T(1,128)} %bitcast.6), custom_call_target="tpu_custom_call" | custom-call | tf_op jit(solution)/shard_map/pallas_call | solution.py:581
  51.9 0.8 %shard_map.95 = (f32[32,4096]{1,0:T(8,128)}, f32[4,16]{1,0:T(4,128)}, f32[1,16]{1,0:T(1,128)}) custom-call(f32[32,4096]{1,0:T(8,128)S(1)} %get-tuple-element.8.value, f32[8,128]{1,0:T(8,128)S(1)} %get-tuple-element.9.small), custom_call_target="tpu_custom_call" | custom-call | tf_op jit(solution)/shard_map/pallas_call | solution.py:644

commit v7 on v6

--- a/solution.py
+++ b/solution.py
@@ -114,16 +114,10 @@
     width = min(1024, paths // CORES)
     pieces = [slice(c, c + width) for c in range(0, paths, width)]
 
-    def each_piece(body, carry=None, unroll=False):
-        if unroll:
-            for c, cut in enumerate(pieces):
-                carry = body(c, cut, carry)
-            return carry
-
-        def one(c, carry):
-            return body(c, pl.ds(pl.multiple_of(c * width, width), width), carry)
-
-        return lax.fori_loop(0, paths // width, one, carry)
+    def each_piece(body, carry=None):
+        for c, cut in enumerate(pieces):
+            carry = body(c, cut, carry)
+        return carry
 
 
     def distance(o):
@@ -231,7 +225,7 @@
 
         each_piece(piece)
 
-    def gram(d, unroll=False):
+    def gram(d):
         height = SLABS * K
 
         def piece(c, cut, total):
@@ -244,7 +238,7 @@
                     products[height * i + K * o : height * i + K * o + K, cut] = part
             return total + dot(products[:, cut], masks[:, cut], NT)
 
-        total = each_piece(piece, jnp.zeros((2 * height, trades), jnp.float32), unroll)
+        total = each_piece(piece, jnp.zeros((2 * height, trades), jnp.float32))
         gram_acc[0:height, 0:trades] = total[0:height] + total[height : 2 * height]
 
     def rhs(parts):
@@ -487,7 +481,7 @@
     rhs_acc[...] = jnp.zeros_like(rhs_acc)
     positive[...] = jnp.zeros_like(positive)
     have(("low", 2), ("high", 2), ("exercise", 2))
-    gram(2, unroll=True)
+    gram(2)
     pl.semaphore_wait(barrier, len(along_path + along_core + along_y + along_z_lo))
     first_sends()
     prepare(2)
@@ -555,14 +549,15 @@
 
 def write_results(value, small, value_out, exposure_out, cva_out, exposure, cva, sems):
     dates = exposure.shape[0]
-    exposure[...] = small[0:dates, 0:NS]
-    cva[...] = small[dates : dates + 1, 0:NS]
     copies = [
         pltpu.make_async_copy(value, value_out, sems.at[0]),
         pltpu.make_async_copy(exposure, exposure_out, sems.at[1]),
         pltpu.make_async_copy(cva, cva_out, sems.at[2]),
     ]
-    for copy in copies:
+    copies[0].start()
+    exposure[...] = small[0:dates, 0:NS]
+    cva[...] = small[dates : dates + 1, 0:NS]
+    for copy in copies[1:]:
         copy.start()
     for copy in copies:
         copy.wait()

time: 52.8 us -> 53.1 us (level)
  no operation moved by 1% of the time
where the time goes in v7:
time: 53.1 us; the launch traced here: 53 us
  Pallas kernels  52.4 us (99%)
  between operations  0.64 us (1%)
    pallas_call x1, Pallas kernels, on_device(): pl.pallas_call(functools.partial(kernel, members), out_shape=(pltpu.VMEM(...  51.5 us

profile of v7, /device:TPU:1, one launch (start us, length us, event | category | flops | bytes accessed | tf_op | source)
XLA Modules:
  0.0 53.0 jit_solution(10486084397236299664)
XLA Ops:
  0.6 51.5 %shard_map.94 = (f32[32,4096]{1,0:T(8,128)S(1)}, f32[8,128]{1,0:T(8,128)S(1)}) custom-call(bf16[4,32,4096]{2,1,0:T(8,128)(2,1)} %exercise_hbm.1, f32[3,16,4096]{2,1,0:T(8,128)} %basis_hbm.1, f32[3,4096]{1,0:T(4,128)} %discount_hbm.1, f32[4,4096]{1,0:T(4,128)} %deflator_hbm.1, f32[1,32]{1,0:T(1,128)} %bitcast.4, s32[1,32]{1,0:T(1,128)} %bitcast.5, f32[1,4]{1,0:T(1,128)} %bitcast.6), custom_call_target="tpu_custom_call" | custom-call | tf_op jit(solution)/shard_map/pallas_call | solution.py:576
  52.2 0.8 %shard_map.95 = (f32[32,4096]{1,0:T(8,128)}, f32[4,16]{1,0:T(4,128)}, f32[1,16]{1,0:T(1,128)}) custom-call(f32[32,4096]{1,0:T(8,128)S(1)} %get-tuple-element.8.value, f32[8,128]{1,0:T(8,128)S(1)} %get-tuple-element.9.small), custom_call_target="tpu_custom_call" | custom-call | tf_op jit(solution)/shard_map/pallas_call | solution.py:639
